TPU v7x, 512 devices: a whole 4x8x8 slice. The times are simulated.
512 devices in a mesh: dom: 512 (over y, x, z, core).
Axes of the slice: x: 4, y: 8, z: 8, core: 2. Of those that a mesh axis runs over, the one named last changes fastest.
Arguments:
- current: float32 [86528, 768], P('dom'), may hold values from -6 to 6
- previous: float32 [86528, 768], P('dom'), may hold values from -6 to 6
- material: bfloat16 [4608, 25, 768], P('dom'), may hold values from 0.5 to 2
- stepping: float32 [86528], P('dom'), may hold values from 0.01 to 0.1
- point_order: int32 [512, 169], P('dom'), may hold values from 0 to 168, each once within a row
- order_bucket: int32 [512, 9], P('dom'), may hold values from 0 to 3
Outputs:
- following: float32 [86528, 768], P('dom')
All inputs are finite; a program needn't handle non-finite values.
Results may differ from a plain program's by a relative error of at most 0.0003.
Values sent between devices are 32-bit elements; how exact they have to be, the bound alone decides.
A program may use at most 64 MiB of HBM per device.

v0:
```python
import functools

import jax
import jax.numpy as jnp
import ml_dtypes
import numpy as np
from jax import lax
from jax.experimental import pallas as pl
from jax.experimental.pallas import tpu as pltpu
from jax.sharding import PartitionSpec as P

ELEM_SIDE = 3
TIME_STEPS = 2
GRID_COLUMNS = 8
SIDE = 4 * ELEM_SIDE + 1
POINTS = SIDE * SIDE
COLS = 768
ELEMS = ELEM_SIDE * ELEM_SIDE
CENTRE = ELEMS // 2
MAIN = 200
ROWS = 240
STORED = 176
HALO = 64

VMEM_GRANT = 48 * 1024 * 1024

MESH = pl.DeviceIdType.MESH
BF16 = jnp.bfloat16
F32 = jnp.float32

ROUTES = (
    (0, 1, 39, 26, 13),
    (0, -1, 26, 39, 13),
    (1, 0, 13, 0, 13),
    (-1, 0, 0, 13, 13),
    (1, 1, 25, 52, 1),
    (-1, 1, 12, 53, 1),
    (1, -1, 13, 54, 1),
    (-1, -1, 0, 55, 1),
)
EDGE_ROWS = 80


def split_np(table):
    high = table.astype(np.float32).astype(ml_dtypes.bfloat16)
    low = (table - high.astype(np.float64)).astype(np.float32).astype(ml_dtypes.bfloat16)
    return np.stack([high, low])


def gll_tables():
    nodes = np.array([-1.0, -np.sqrt(3.0 / 7.0), 0.0, np.sqrt(3.0 / 7.0), 1.0])
    weights = np.array([0.1, 49.0 / 90.0, 32.0 / 45.0, 49.0 / 90.0, 0.1])
    bary = np.array([1.0 / np.prod([nodes[j] - nodes[k] for k in range(5) if k != j]) for j in range(5)])
    derivative = np.zeros((5, 5))
    for i in range(5):
        for j in range(5):
            if i != j:
                derivative[i, j] = bary[j] / bary[i] / (nodes[i] - nodes[j])
        derivative[i, i] = -np.sum(derivative[i])
    return derivative, np.outer(weights, weights)


SHAPES = ((ROWS, STORED), (STORED, 2 * HALO), (EDGE_ROWS, STORED), (EDGE_ROWS, 2 * HALO), (64, 96), (32, 192), (HALO, 2 * EDGE_ROWS))
PACKED = tuple((sum(r for r, _ in SHAPES[:i]), rows, columns) for i, (rows, columns) in enumerate(SHAPES))
PACKED_ROWS = sum(r for r, _ in SHAPES)

DERIV, QUAD = gll_tables()
ODD = [[float(DERIV[i, j] - DERIV[i, 4 - j]) / 2 for j in range(2)] for i in range(2)]
EVEN = [[float(DERIV[i, j] + DERIV[i, 4 - j]) / 2 for j in range(2)] for i in range(2)]
MIDDLE = [float(DERIV[2, j]) for j in range(2)]
ODD_T = [[float(DERIV[c, a] - DERIV[4 - c, a]) / 2 for c in range(2)] for a in range(2)]
EVEN_T = [[float(DERIV[c, a] + DERIV[4 - c, a]) / 2 for c in range(2)] + [float(DERIV[2, a])] for a in range(2)]
MIDDLE_T = [float(DERIV[c, 2]) for c in range(2)]


BLOCKS = ((0, 0), (1, 0), (0, 1), (0, 2), (1, 1), (1, 2))


def block_columns(parity, kind):
    lane = np.arange(128)
    half = (lane % 4) // 2
    source = lane + 2 * (parity - half)
    return 128 * ((kind - (source // 2) % 3) % 3 + 3 * half) + source


def stacked(table):
    high, low = split_np(table)
    return np.concatenate([high, high, low])


def squared(table):
    high, low = split_np(table)
    return np.concatenate([np.concatenate([high, low], axis=1), np.concatenate([high, 0 * low], axis=1)])


def transform_tables():
    sample = np.arange(128)

    def parts(parity, kind):
        column = block_columns(parity, kind)
        order = column // 2
        angle = (order[:, None] * sample[None, :] % COLS) * (2.0 * np.pi / COLS)
        even = (column % 2 == 0)[:, None]
        real = np.where(even, np.cos(angle), np.sin(angle))
        turned = np.where(even, -np.sin(angle), np.cos(angle)) * (np.sqrt(3.0) / 2.0)
        scale = np.where(order == 0, 1.0, 2.0) / COLS
        return real, turned, scale[:, None]

    tables = [[], [], [], []]
    for parity in range(2):
        real, _, scale = parts(parity, 0)
        tables[0].append(squared(real))
        tables[2].append(squared((real * scale).T))
        real1, turned1, scale1 = parts(parity, 1)
        real2, turned2, scale2 = parts(parity, 2)
        real, scale = np.concatenate([real1, real2]), np.concatenate([scale1, scale2])
        both = np.concatenate([real, np.concatenate([turned1, -turned2])], axis=1)
        tables[1].append(stacked(both))
        tables[3].append(stacked((both * scale).T))
    return np.concatenate(tables[0] + tables[1]), np.concatenate(tables[2] + tables[3])


def row_places():
    elem, point = np.full(ROWS, -1), np.full(ROWS, 0)
    outer = [e for e in range(ELEMS) if e != CENTRE]
    elem[:MAIN] = np.tile(outer, 25)
    point[:MAIN] = np.repeat(np.arange(25), 8)
    elem[MAIN : MAIN + 25] = CENTRE
    point[MAIN : MAIN + 25] = np.arange(25)
    return elem, point


def static_tables():
    elem, point = row_places()
    a, b = point // 5, point % 5
    used = elem >= 0
    struct = np.where(used, (4 * (elem // ELEM_SIDE) + a) * SIDE + 4 * (elem % ELEM_SIDE) + b, -1)
    gather = (np.arange(POINTS)[:, None] == struct[None, :]).astype(np.float64)
    gather = np.concatenate([gather, np.zeros((STORED - POINTS, ROWS))])
    place = np.zeros((STORED, HALO))
    along = np.arange(SIDE)
    edges = (along, 12 * SIDE + along, along * SIDE, along * SIDE + 12)
    corners = (0, 12 * SIDE, 12, 12 * SIDE + 12)
    for slot, (edge, corner) in enumerate(zip(edges, corners)):
        place[edge, SIDE * slot + along] = 1.0
        place[corner, 4 * SIDE + slot] = 1.0

    five = np.arange(25)
    fa, fb = five // 5, five % 5
    first = np.where(fb[:, None] == fb[None, :], DERIV[fa[:, None], fa[None, :]], 0.0)
    second = np.where(fa[:, None] == fa[None, :], DERIV[fb[:, None], fb[None, :]], 0.0)
    slope = np.zeros((64, 32))
    slope[:25, :25] = first
    slope[32:57, :25] = second
    weight = np.zeros(64)
    weight[:25] = weight[32:57] = QUAD[fa, fb]

    def across(table):
        high, low = split_np(table)
        return np.concatenate([high, low, high], axis=1)

    rim = np.full(EDGE_ROWS, -1)
    outer = [e for e in range(ELEMS) if e != CENTRE]
    for i in range(5):
        for q, e in enumerate(outer):
            ex, ey = e // ELEM_SIDE, e % ELEM_SIDE
            if ex != 1:
                rim[8 * i + q] = (4 * ex + 2 * ex) * SIDE + 4 * ey + i
            covered = (ex == 0 and i == 0) or (ex == 2 and i == 4)
            if ey != 1 and not covered:
                rim[40 + 8 * i + q] = (4 * ex + i) * SIDE + 6 * ey
    outgoing = np.zeros((HALO, EDGE_ROWS))
    for slot, edge in enumerate(edges):
        outgoing[SIDE * slot : SIDE * slot + SIDE] = edge[:, None] == rim[None, :]
    rim_gather = (rim[:, None] == np.arange(STORED)[None, :]).astype(np.float64)

    twice = lambda table: np.concatenate([table, table], axis=1)
    packed = np.zeros((PACKED_ROWS, 256), ml_dtypes.bfloat16)
    for (first, rows, columns), table in zip(
        PACKED,
        (
            gather.T,
            twice(place),
            rim_gather,
            twice(rim_gather @ place),
            across(slope),
            across(slope.T * weight[None, :]),
            twice(outgoing),
        ),
    ):
        packed[first : first + rows, :columns] = table.astype(ml_dtypes.bfloat16)
    return packed, twice(gather).astype(ml_dtypes.bfloat16)


def split(value):
    high = value.astype(BF16)
    return high, (value - high.astype(F32)).astype(BF16)


def dot(left, right):
    return jnp.dot(left, right, preferred_element_type=F32)


def slope_line(u):
    odd0, odd1, twice = u[0] - u[4], u[1] - u[3], u[2] + u[2]
    even0, even1 = u[0] + u[4] - twice, u[1] + u[3] - twice
    plus, minus = [], []
    for i in range(2):
        plus.append(ODD[i][0] * odd0 + ODD[i][1] * odd1)
        minus.append(EVEN[i][0] * even0 + EVEN[i][1] * even1)
    middle = MIDDLE[0] * odd0 + MIDDLE[1] * odd1
    return [plus[0] + minus[0], plus[1] + minus[1], middle, plus[1] - minus[1], plus[0] - minus[0]]


def force_line(s):
    odd0, odd1 = s[0] - s[4], s[1] - s[3]
    even0, even1 = s[0] + s[4], s[1] + s[3]
    plus, minus = [], []
    for a in range(2):
        plus.append(ODD_T[a][0] * odd0 + ODD_T[a][1] * odd1)
        minus.append(EVEN_T[a][0] * even0 + EVEN_T[a][1] * even1 + EVEN_T[a][2] * s[2])
    middle = MIDDLE_T[0] * odd0 + MIDDLE_T[1] * odd1
    return [plus[0] + minus[0], plus[1] + minus[1], middle, plus[1] - minus[1], plus[0] - minus[0]]


def by_class(value, lane):
    kind_of_lane, early = lax.rem(lane // 2, 3), lax.rem(lane, 4) < 2
    slabs = [value[:, 128 * v : 128 * v + 128] for v in range(6)]
    blocks = {}
    for kind in range(3):
        first, second = [
            jnp.where(
                kind_of_lane == 0,
                slabs[kind + 3 * h],
                jnp.where(kind_of_lane == 1, slabs[(kind - 1) % 3 + 3 * h], slabs[(kind - 2) % 3 + 3 * h]),
            )
            for h in range(2)
        ]
        blocks[0, kind] = jnp.where(early, first, pltpu.roll(second, 2, 1))
        blocks[1, kind] = jnp.where(early, pltpu.roll(first, 126, 1), second)
    return jnp.concatenate([blocks[block] for block in BLOCKS], axis=1)


def by_column(value, lane):
    kind_of_lane, early = lax.rem(lane // 2, 3), lax.rem(lane, 4) < 2
    blocks = {block: value[:, 128 * i : 128 * i + 128] for i, block in enumerate(BLOCKS)}
    halves = [[], []]
    for kind in range(3):
        even, odd = blocks[0, kind], blocks[1, kind]
        halves[0].append(jnp.where(early, even, pltpu.roll(odd, 2, 1)))
        halves[1].append(jnp.where(early, pltpu.roll(even, 126, 1), odd))
    slabs = []
    for v in range(6):
        parts = halves[v // 3]
        slabs.append(
            jnp.where(
                kind_of_lane == 0, parts[v % 3], jnp.where(kind_of_lane == 1, parts[(v + 1) % 3], parts[(v + 2) % 3])
            )
        )
    return jnp.concatenate(slabs, axis=1)


def class_sums(high, low, table):
    first, others = [], []
    for parity in range(2):
        lanes = slice(128 * parity, 128 * parity + 128)
        both = dot(
            jnp.concatenate([high[:, lanes], low[:, lanes]], axis=1), table[256 * parity : 256 * parity + 256, :]
        )
        first.append(both[:, 0:128] + both[:, 128:256])
    for parity in range(2):
        lanes = slice(256 + 256 * parity, 512 + 256 * parity)
        others.append(
            dot(
                jnp.concatenate([high[:, lanes], low[:, lanes], high[:, lanes]], axis=1),
                table[512 + 768 * parity : 1280 + 768 * parity, :],
            )
        )
    return first, others


def sample_blocks(bases, boths):
    parities = []
    for base, both in zip(bases, boths):
        real, turned = both[:, 0:128], both[:, 128:256]
        half = base - 0.5 * real
        parities.append((base + real, half + turned, half - turned))
    out = [None] * 6
    for t in range(3):
        out[2 * t] = parities[0][t] + parities[1][t]
        out[(2 * t + 3) % 6] = parities[0][t] - parities[1][t]
    return out


def coefficients(forces, table):
    out0, out12 = [], []
    for sign in (1, -1):
        parts = []
        for t in range(3):
            one, other = forces[2 * t], forces[(2 * t + 3) % 6]
            parts.append(one + other if sign > 0 else one - other)
        pair = parts[1] + parts[2]
        out0.append(parts[0] + pair)
        out12 += [parts[0] - 0.5 * pair, parts[1] - parts[2]]
    first, others = class_sums(*split(jnp.concatenate(out0 + out12, axis=1)), table)
    return jnp.concatenate(first + others, axis=1)


def rim_tiles(forces, c, picks):
    tiles = []
    for low, high, step, span in ((picks[0], picks[1], 1, 20), (picks[2], picks[3], 5, 4)):
        for i in range(5):
            p = step * i
            one, other = forces[c, 8 * p : 8 * p + 8, :], forces[c, 8 * (p + span) : 8 * (p + span) + 8, :]
            tiles.append(jnp.where(low, one, jnp.where(high, other, 0.0)))
    return jnp.concatenate(tiles, axis=0)


def slope_line(u):
    odd0, odd1, twice = u[0] - u[4], u[1] - u[3], u[2] + u[2]
    even0, even1 = u[0] + u[4] - twice, u[1] + u[3] - twice
    plus, minus = [], []
    for i in range(2):
        plus.append(ODD[i][0] * odd0 + ODD[i][1] * odd1)
        minus.append(EVEN[i][0] * even0 + EVEN[i][1] * even1)
    middle = MIDDLE[0] * odd0 + MIDDLE[1] * odd1
    return [plus[0] + minus[0], plus[1] + minus[1], middle, plus[1] - minus[1], plus[0] - minus[0]]


def force_line(s):
    odd0, odd1 = s[0] - s[4], s[1] - s[3]
    even0, even1 = s[0] + s[4], s[1] + s[3]
    plus, minus = [], []
    for a in range(2):
        plus.append(ODD_T[a][0] * odd0 + ODD_T[a][1] * odd1)
        minus.append(EVEN_T[a][0] * even0 + EVEN_T[a][1] * even1 + EVEN_T[a][2] * s[2])
    middle = MIDDLE_T[0] * odd0 + MIDDLE_T[1] * odd1
    return [plus[0] + minus[0], plus[1] + minus[1], middle, plus[1] - minus[1], plus[0] - minus[0]]


def by_class(value, lane):
    kind_of_lane, early = lax.rem(lane // 2, 3), lax.rem(lane, 4) < 2
    slabs = [value[:, 128 * v : 128 * v + 128] for v in range(6)]
    blocks = {}
    for kind in range(3):
        first, second = [
            jnp.where(
                kind_of_lane == 0,
                slabs[kind + 3 * h],
                jnp.where(kind_of_lane == 1, slabs[(kind - 1) % 3 + 3 * h], slabs[(kind - 2) % 3 + 3 * h]),
            )
            for h in range(2)
        ]
        blocks[0, kind] = jnp.where(early, first, pltpu.roll(second, 2, 1))
        blocks[1, kind] = jnp.where(early, pltpu.roll(first, 126, 1), second)
    return jnp.concatenate([blocks[block] for block in BLOCKS], axis=1)


def by_column(value, lane):
    kind_of_lane, early = lax.rem(lane // 2, 3), lax.rem(lane, 4) < 2
    blocks = {block: value[:, 128 * i : 128 * i + 128] for i, block in enumerate(BLOCKS)}
    halves = [[], []]
    for kind in range(3):
        even, odd = blocks[0, kind], blocks[1, kind]
        halves[0].append(jnp.where(early, even, pltpu.roll(odd, 2, 1)))
        halves[1].append(jnp.where(early, pltpu.roll(even, 126, 1), odd))
    slabs = []
    for v in range(6):
        parts = halves[v // 3]
        slabs.append(
            jnp.where(
                kind_of_lane == 0, parts[v % 3], jnp.where(kind_of_lane == 1, parts[(v + 1) % 3], parts[(v + 2) % 3])
            )
        )
    return jnp.concatenate(slabs, axis=1)


def class_sums(high, low, table):
    first, others = [], []
    for parity in range(2):
        lanes = slice(128 * parity, 128 * parity + 128)
        both = dot(
            jnp.concatenate([high[:, lanes], low[:, lanes]], axis=1), table[256 * parity : 256 * parity + 256, :]
        )
        first.append(both[:, 0:128] + both[:, 128:256])
    for parity in range(2):
        lanes = slice(256 + 256 * parity, 512 + 256 * parity)
        others.append(
            dot(
                jnp.concatenate([high[:, lanes], low[:, lanes], high[:, lanes]], axis=1),
                table[512 + 768 * parity : 1280 + 768 * parity, :],
            )
        )
    return first, others


def sample_blocks(bases, boths):
    parities = []
    for base, both in zip(bases, boths):
        real, turned = both[:, 0:128], both[:, 128:256]
        half = base - 0.5 * real
        parities.append((base + real, half + turned, half - turned))
    out = [None] * 6
    for t in range(3):
        out[2 * t] = parities[0][t] + parities[1][t]
        out[(2 * t + 3) % 6] = parities[0][t] - parities[1][t]
    return out


def force_sums(forces):
    out0, out12 = [], []
    for sign in (1, -1):
        parts = []
        for t in range(3):
            one, other = forces[2 * t, :, :], forces[(2 * t + 3) % 6, :, :]
            parts.append(one + other if sign > 0 else one - other)
        pair = parts[1] + parts[2]
        out0.append(parts[0] + pair)
        out12.append(jnp.concatenate([parts[0] - 0.5 * pair, parts[1] - parts[2]], axis=1))
    return jnp.concatenate(out0, axis=1), jnp.concatenate(out12, axis=1)


def outer_forces(samples, modulus, forces):
    def one_block(c, carry):
        u = [samples[c, 8 * p : 8 * p + 8, :] for p in range(25)]
        total = [None] * 25
        for b in range(5):
            places = [5 * a + b for a in range(5)]
            slopes = slope_line([u[p] for p in places])
            stress = [slopes[a] * modulus[c, 8 * p : 8 * p + 8, :] for a, p in enumerate(places)]
            for p, part in zip(places, force_line(stress)):
                total[p] = part
        for a in range(5):
            places = [5 * a + b for b in range(5)]
            slopes = slope_line([u[p] for p in places])
            stress = [slopes[b] * modulus[c, 8 * p : 8 * p + 8, :] for b, p in enumerate(places)]
            for p, part in zip(places, force_line(stress)):
                forces[c, 8 * p : 8 * p + 8, :] = total[p] + part
        return carry

    lax.fori_loop(0, 6, one_block, 0)


def padded(ref):
    first = lax.broadcasted_iota(jnp.int32, (8, COLS), 0) == 0
    return jnp.concatenate([ref[0:168, :], jnp.where(first, ref[168:169, :], 0.0)], axis=0)


def slabs_of(ref, first, count):
    return jnp.concatenate([ref[c, first : first + count, :] for c in range(6)], axis=1)


def kernel(rows_total, *refs):
    sources, out_ref, held, refs = refs[:10], refs[10], refs[11:21], refs[21:]
    (order_pad, step_pad, mat, mat_centre, samples, forces, keep, field, partial) = refs[:9]
    (scales, collect_ref, assemble, settle, send, recv, load_sem, send_sem, recv_sem) = refs[9:]
    cur, order, packed, bucket, inverse, mat_in, forward, stepping, gather, prev = held

    me = lax.axis_index("dom")
    column = lax.rem(me, GRID_COLUMNS)
    row = lax.div(me, GRID_COLUMNS)

    loads = [pltpu.make_async_copy(sources[i], held[i], load_sem.at[i]) for i in range(10)]
    for load in loads:
        load.start()

    recv[...] = jnp.zeros_like(recv)

    def exists(dc, dr):
        c, r = column + dc, row + dr
        return (c >= 0) & (c < GRID_COLUMNS) & (r >= 0) & (r < rows_total)

    barrier = pltpu.get_barrier_semaphore()
    expected = jnp.int32(0)
    for dc, dr, _, _, _ in ROUTES:
        here = exists(dc, dr)
        expected = expected + here.astype(jnp.int32)

        @pl.when(here)
        def _():
            pl.semaphore_signal(barrier, inc=1, device_id=(me + dc + GRID_COLUMNS * dr,), device_id_type=MESH)

    order_pad[...] = jnp.full(order_pad.shape, -1, jnp.int32)
    step_pad[...] = jnp.zeros_like(step_pad)
    forces[:, MAIN + 32 : ROWS, :] = jnp.zeros((6, ROWS - MAIN - 32, 128), F32)
    mat_centre[...] = jnp.zeros_like(mat_centre)
    lane = lax.broadcasted_iota(jnp.int32, (1, 128), 1)
    q = lax.broadcasted_iota(jnp.int32, (8, 128), 0)
    picks = (q < 3, q >= 5, (q == 0) | (q == 3) | (q == 5), (q == 2) | (q == 4) | (q == 7))

    place_at = lax.broadcasted_iota(jnp.int32, (1, COLS), 1)
    block, inside = place_at >> 7, place_at & 127
    parity = ((block == 1) | (block >= 4)).astype(jnp.int32)
    kind = jnp.where(block < 2, 0, jnp.where((block == 2) | (block == 4), 1, 2))
    half = (inside >> 1) & 1
    source = inside + 2 * (parity - half)
    natural = (128 * (lax.rem(kind + 3 - lax.rem(source >> 1, 3), 3) + 3 * half) + source).astype(F32)

    def table(i):
        first, rows, columns = PACKED[i]
        return packed[first : first + rows, 0:columns]

    loads[1].wait()
    order_pad[0:1, 0:POINTS] = order[...]
    stored_row = lax.broadcasted_iota(jnp.int32, (STORED, STORED), 0)
    one_hot = jnp.where(stored_row == order_pad[0:1, :], 1.0, 0.0).astype(BF16)

    def stored_of(selection):
        return lax.dot_general(selection, one_hot, (((1,), (1,)), ((), ())), preferred_element_type=F32)

    loads[2].wait()
    collect = stored_of(table(0)).astype(BF16)

    loads[3].wait()
    limit_row = lax.shift_right_logical(jnp.full((1, ELEMS), COLS, jnp.int32), 3 - bucket[...]).astype(F32)
    elem_row = lax.broadcasted_iota(jnp.int32, (ROWS, ELEMS), 0)
    inner = lax.rem(elem_row, 8)
    owner = jnp.where(elem_row < MAIN, inner + (inner >= CENTRE).astype(jnp.int32), CENTRE)
    owned = owner == lax.broadcasted_iota(jnp.int32, (ROWS, ELEMS), 1)
    limit_col = jnp.sum(jnp.where(owned, limit_row, 0.0), axis=1, keepdims=True)
    keep[...] = jnp.where(natural < limit_col, 1.0, 0.0).astype(BF16)

    collect_ref[...] = collect
    loads[0].wait()
    field[...] = by_class(padded(cur), lane)
    partial[...] = field[...]

    def exchange(step):
        return [
            (
                pltpu.make_async_remote_copy(
                    src_ref=send.at[step, pl.ds(source, rows)],
                    dst_ref=recv.at[step, pl.ds(target, rows)],
                    send_sem=send_sem.at[step, d],
                    recv_sem=recv_sem.at[step, d],
                    device_id=(me + dc + GRID_COLUMNS * dr,),
                    device_id_type=MESH,
                ),
                exists(dc, dr),
                exists(-dc, -dr),
            )
            for d, (dc, dr, source, target, rows) in enumerate(ROUTES)
        ]

    def arrived(step):
        for copy, _, comes in exchange(step):
            pl.when(comes)(copy.wait_recv)
        return recv[step].reshape(HALO, COLS)

    def one_step(step, carry):
        high, low = [dot(collect_ref[...], half).astype(BF16) * keep[...] for half in split(partial[...])]

        @pl.when(step == 0)
        def _():
            loads[4].wait()

        for c, value in enumerate(sample_blocks(*class_sums(high, low, inverse))):
            samples[c, :, :] = value

        @pl.when(step == 0)
        def _():
            loads[5].wait()
            for e in range(ELEMS):
                if e == CENTRE:
                    mat_centre[0:25, :] = mat_in[e].astype(F32)
                else:
                    for c in range(6):
                        values = mat_in[e, :, 128 * c : 128 * c + 128].astype(F32)
                        mat[c, pl.ds(e - (e > CENTRE), 25, stride=8), :] = values
            for p in range(25):
                mat[:, 8 * p : 8 * p + 8, :] = mat[:, 8 * p : 8 * p + 8, :] * float(QUAD[p // 5, p % 5])
            loads[6].wait()

        @pl.when(step > 0)
        def _():
            rim = dot(table(3), jnp.concatenate(split(arrived(0)), axis=0))
            rim = jnp.where(natural < limit_col[0:EDGE_ROWS], -scales[STORED : STORED + EDGE_ROWS, 0:1] * rim, 0.0)
            for c, value in enumerate(sample_blocks(*class_sums(*split(rim), inverse))):
                for i in range(5):
                    for at, ends in (
                        (8 * i, ((i, picks[0]), (20 + i, picks[1]))),
                        (40 + 8 * i, ((5 * i, picks[2]), (5 * i + 4, picks[3]))),
                    ):
                        tile = value[at : at + 8, :]
                        for p, chosen in ends:
                            samples[c, 8 * p : 8 * p + 8, :] = samples[c, 8 * p : 8 * p + 8, :] + jnp.where(
                                chosen, tile, 0.0
                            )

        outer_forces(samples, mat, forces)
        value = coefficients([rim_tiles(forces, c, picks) for c in range(6)], forward)
        value = jnp.where(natural < limit_col[0:EDGE_ROWS], value, 0.0)
        edges = dot(table(6), jnp.concatenate(split(value), axis=0))
        send[step] = edges.reshape(HALO, 1, COLS)

        @pl.when(step == 0)
        def _():
            pl.semaphore_wait(barrier, expected)

        for copy, goes, _ in exchange(step):
            pl.when(goes)(copy.start)

        high, low = split(slabs_of(samples, MAIN, 32))
        slopes = dot(table(4), jnp.concatenate([high, high, low], axis=0))
        modulus = mat_centre[...]
        high, low = split(jnp.concatenate([slopes[:32] * modulus, slopes[32:] * modulus], axis=0))
        centre = dot(table(5), jnp.concatenate([high, high, low], axis=0))
        for c in range(6):
            forces[c, MAIN : MAIN + 32, :] = centre[:, 128 * c : 128 * c + 128]
        value = coefficients([forces[c, :, :] for c in range(6)], forward)
        coefs = jnp.concatenate(split(jnp.where(natural < limit_col, value, 0.0)), axis=0)

        @pl.when(step == 0)
        def _():
            for load in loads[7:]:
                load.wait()
            step_pad[0:1, 0:POINTS] = stepping[...]
            step_row = step_pad[0:1, :]
            diagonal = stored_row == lax.broadcasted_iota(jnp.int32, (STORED, STORED), 1)
            step_col = jnp.sum(jnp.where(diagonal, step_row, 0.0), axis=1, keepdims=True)
            scales[0:STORED, :] = jnp.broadcast_to(step_col, (STORED, 128))
            rim_step = jnp.sum(stored_of(table(2)) * step_row, axis=1, keepdims=True)
            scales[STORED:, :] = jnp.broadcast_to(rim_step, (EDGE_ROWS, 128))
            assemble[...] = dot(one_hot, gather[...]).astype(BF16)
            settle[...] = dot(one_hot, table(1)).astype(BF16)
            partial[...] = 2.0 * field[...] - by_class(padded(prev), lane)

        @pl.when(step > 0)
        def _():
            settled = dot(settle[...], jnp.concatenate(split(recv[0].reshape(HALO, COLS)), axis=0))
            partial[...] = 2.0 * (partial[...] - scales[0:STORED, 0:1] * settled) - field[...]

        partial[...] = partial[...] - scales[0:STORED, 0:1] * dot(assemble[...], coefs)
        return carry

    lax.fori_loop(0, TIME_STEPS, one_step, 0)
    last = by_column(partial[...], lane)
    settled = dot(settle[...], jnp.concatenate(split(by_column(arrived(TIME_STEPS - 1), lane)), axis=0))
    out_ref[...] = (last - scales[0:STORED, 0:1] * settled)[0:POINTS]
    for step in range(TIME_STEPS):
        for copy, goes, _ in exchange(step):
            pl.when(goes)(copy.wait_send)


def solution(mesh):
    rows_total = mesh.shape["dom"] // GRID_COLUMNS
    inverse, forward = transform_tables()
    packed, gather = static_tables()

    def local(current, previous, material, stepping, point_order, order_bucket):
        operands = [
            current,
            point_order,
            packed,
            order_bucket,
            inverse,
            material,
            forward,
            stepping.reshape(1, POINTS),
            gather,
            previous,
        ]
        operands = [
            pltpu.with_memory_space_constraint(jnp.asarray(operand), pltpu.HBM) for operand in operands
        ]
        return pl.pallas_call(
            functools.partial(kernel, rows_total),
            out_shape=jax.ShapeDtypeStruct((POINTS, COLS), F32),
            in_specs=[pl.BlockSpec(memory_space=pltpu.HBM)] * len(operands),
            out_specs=pl.BlockSpec(memory_space=pltpu.VMEM),
            scratch_shapes=[pltpu.VMEM(operand.shape, operand.dtype) for operand in operands]
            + [
                pltpu.VMEM((8, STORED), jnp.int32),
                pltpu.VMEM((8, STORED), F32),
                pltpu.VMEM((6, MAIN, 128), F32),
                pltpu.VMEM((32, COLS), F32),
                pltpu.VMEM((6, ROWS, 128), F32),
                pltpu.VMEM((6, ROWS, 128), F32),
                pltpu.VMEM((ROWS, COLS), BF16),
                pltpu.VMEM((STORED, COLS), F32),
                pltpu.VMEM((STORED, COLS), F32),
                pltpu.VMEM((STORED + EDGE_ROWS, 128), F32),
                pltpu.VMEM((ROWS, STORED), BF16),
                pltpu.VMEM((STORED, 2 * ROWS), BF16),
                pltpu.VMEM((STORED, 2 * HALO), BF16),
                pltpu.VMEM((TIME_STEPS, HALO, 1, COLS), F32),
                pltpu.VMEM((TIME_STEPS, HALO, 1, COLS), F32),
                pltpu.SemaphoreType.DMA((len(operands),)),
                pltpu.SemaphoreType.DMA((TIME_STEPS, 8)),
                pltpu.SemaphoreType.DMA((TIME_STEPS, 8)),
            ],
            compiler_params=pltpu.CompilerParams(
                collective_id=0, has_side_effects=True, vmem_limit_bytes=VMEM_GRANT
            ),
        )(*operands)

    return jax.shard_map(
        local,
        mesh=mesh,
        in_specs=(
            P("dom", None),
            P("dom", None),
            P("dom", None, None),
            P("dom"),
            P("dom", None),
            P("dom", None),
        ),
        out_specs=P("dom", None),
        check_vma=False,
    )
```

profile of v0, /device:TPU:48, one launch (start us, length us, event | category | flops | bytes accessed | tf_op | source)
XLA Modules:
  0.0 31.7 jit_solution(12763679511591755461)
XLA Ops:
  0.0 30.9 %shard_map.100 = f32[169,768]{1,0:T(8,128)S(1)} custom-call(f32[169,768]{1,0:T(8,128)} %refs_0_.1, s32[1,169]{1,0:T(1,128)} %refs_1_.1, bf16[736,256]{1,0:T(8,128)(2,1)} %constant.8.clone.refs_2_, s32[1,9]{1,0:T(1,128)} %refs_3_.1, bf16[2048,256]{1,0:T(8,128)(2,1)} %constant.9.clone.refs_4_, bf16[9,25,768]{2,1,0:T(8,128)(2,1)} %refs_5_.1, ...), custom_call_target="tpu_custom_call" | custom-call | tf_op jit(solution)/shard_map/pallas_call | solution.py:666
  30.9 0.8 %copy.12 = f32[169,768]{1,0:T(8,128)} copy(f32[169,768]{1,0:T(8,128)S(1)} %shard_map.100) | data formatting | bytes 1038336
where the time goes:
time: 32.1 us; the launch traced here: 31.7 us
  Pallas kernels  30.9 us (96%)
  local copies, waits for them, and re-layouts  0.8 us (2%)
    pallas_call x1, Pallas kernels, local(): pl.pallas_call(functools.partial(kernel, rows_total), out_shape=jax.Shape...  30.9 us
    unnamed x1, local copies, waits for them, and re-layouts  0.8 us

commit v1 on v0

--- a/solution.py
+++ b/solution.py
@@ -20,7 +20,7 @@
 MAIN = 200
 ROWS = 240
 STORED = 176
-HALO = 64
+HALO = 80
 
 VMEM_GRANT = 48 * 1024 * 1024
 
@@ -28,15 +28,16 @@
 BF16 = jnp.bfloat16
 F32 = jnp.float32
 
+MESSAGE_ROWS = 384
 ROUTES = (
-    (0, 1, 39, 26, 13),
-    (0, -1, 26, 39, 13),
-    (1, 0, 13, 0, 13),
-    (-1, 0, 0, 13, 13),
-    (1, 1, 25, 52, 1),
-    (-1, 1, 12, 53, 1),
-    (1, -1, 13, 54, 1),
-    (-1, -1, 0, 55, 1),
+    (1, 1, 344, 320, 8),
+    (-1, 1, 336, 328, 8),
+    (1, -1, 328, 336, 8),
+    (-1, -1, 320, 344, 8),
+    (0, 1, 240, 160, 80),
+    (0, -1, 160, 240, 80),
+    (1, 0, 80, 0, 80),
+    (-1, 0, 0, 80, 80),
 )
 EDGE_ROWS = 80
 
@@ -142,8 +143,8 @@
     edges = (along, 12 * SIDE + along, along * SIDE, along * SIDE + 12)
     corners = (0, 12 * SIDE, 12, 12 * SIDE + 12)
     for slot, (edge, corner) in enumerate(zip(edges, corners)):
-        place[edge, SIDE * slot + along] = 1.0
-        place[corner, 4 * SIDE + slot] = 1.0
+        place[edge, 16 * slot + along] = 1.0
+        place[corner, 64 + slot] = 1.0
 
     five = np.arange(25)
     fa, fb = five // 5, five % 5
@@ -170,8 +171,9 @@
             if ey != 1 and not covered:
                 rim[40 + 8 * i + q] = (4 * ex + i) * SIDE + 6 * ey
     outgoing = np.zeros((HALO, EDGE_ROWS))
-    for slot, edge in enumerate(edges):
-        outgoing[SIDE * slot : SIDE * slot + SIDE] = edge[:, None] == rim[None, :]
+    for slot, (edge, corner) in enumerate(zip(edges, corners)):
+        outgoing[16 * slot : 16 * slot + SIDE] = edge[:, None] == rim[None, :]
+        outgoing[64 + slot] = corner == rim
     rim_gather = (rim[:, None] == np.arange(STORED)[None, :]).astype(np.float64)
 
     twice = lambda table: np.concatenate([table, table], axis=1)
@@ -461,10 +463,13 @@
     row = lax.div(me, GRID_COLUMNS)
 
     loads = [pltpu.make_async_copy(sources[i], held[i], load_sem.at[i]) for i in range(10)]
-    for load in loads:
-        load.start()
+    for i in (1, 2, 0, 3, 5, 4):
+        loads[i].start()
 
     recv[...] = jnp.zeros_like(recv)
+    for e in range(4):
+        send[:, 80 * e + 72 : 80 * e + 80, :] = jnp.zeros((TIME_STEPS, 8, 128), F32)
+    send[:, 320:352, :] = jnp.zeros((TIME_STEPS, 32, 128), F32)
 
     def exists(dc, dr):
         c, r = column + dc, row + dr
@@ -524,6 +529,18 @@
     loads[0].wait()
     field[...] = by_class(padded(cur), lane)
     partial[...] = field[...]
+    for load in loads[6:]:
+        load.start()
+    loads[5].wait()
+    for e in range(ELEMS):
+        if e == CENTRE:
+            mat_centre[0:25, :] = mat_in[e].astype(F32)
+        else:
+            for c in range(6):
+                values = mat_in[e, :, 128 * c : 128 * c + 128].astype(F32)
+                mat[c, pl.ds(e - (e > CENTRE), 25, stride=8), :] = values
+    for p in range(25):
+        mat[:, 8 * p : 8 * p + 8, :] = mat[:, 8 * p : 8 * p + 8, :] * float(QUAD[p // 5, p % 5])
 
     def exchange(step):
         return [
@@ -542,10 +559,18 @@
             for d, (dc, dr, source, target, rows) in enumerate(ROUTES)
         ]
 
+    def halo_rows(step):
+        columns = []
+        for c in range(6):
+            tiles = [recv[step, pl.ds(80 * e + c, 16, stride=6), :] for e in range(4)]
+            tiles += [recv[step, pl.ds(320 + c, 8, stride=8), :], jnp.zeros((8, 128), F32)]
+            columns.append(jnp.concatenate(tiles, axis=0))
+        return jnp.concatenate(columns, axis=1)
+
     def arrived(step):
         for copy, _, comes in exchange(step):
             pl.when(comes)(copy.wait_recv)
-        return recv[step].reshape(HALO, COLS)
+        return halo_rows(step)
 
     def one_step(step, carry):
         high, low = [dot(collect_ref[...], half).astype(BF16) * keep[...] for half in split(partial[...])]
@@ -559,16 +584,6 @@
 
         @pl.when(step == 0)
         def _():
-            loads[5].wait()
-            for e in range(ELEMS):
-                if e == CENTRE:
-                    mat_centre[0:25, :] = mat_in[e].astype(F32)
-                else:
-                    for c in range(6):
-                        values = mat_in[e, :, 128 * c : 128 * c + 128].astype(F32)
-                        mat[c, pl.ds(e - (e > CENTRE), 25, stride=8), :] = values
-            for p in range(25):
-                mat[:, 8 * p : 8 * p + 8, :] = mat[:, 8 * p : 8 * p + 8, :] * float(QUAD[p // 5, p % 5])
             loads[6].wait()
 
         @pl.when(step > 0)
@@ -591,7 +606,11 @@
         value = coefficients([rim_tiles(forces, c, picks) for c in range(6)], forward)
         value = jnp.where(natural < limit_col[0:EDGE_ROWS], value, 0.0)
         edges = dot(table(6), jnp.concatenate(split(value), axis=0))
-        send[step] = edges.reshape(HALO, 1, COLS)
+        for c in range(6):
+            values = edges[:, 128 * c : 128 * c + 128]
+            for e in range(4):
+                send[step, pl.ds(80 * e + c, SIDE, stride=6), :] = values[16 * e : 16 * e + SIDE]
+            send[step, pl.ds(320 + c, 4, stride=8), :] = values[64:68]
 
         @pl.when(step == 0)
         def _():
@@ -627,7 +646,7 @@
 
         @pl.when(step > 0)
         def _():
-            settled = dot(settle[...], jnp.concatenate(split(recv[0].reshape(HALO, COLS)), axis=0))
+            settled = dot(settle[...], jnp.concatenate(split(halo_rows(0)), axis=0))
             partial[...] = 2.0 * (partial[...] - scales[0:STORED, 0:1] * settled) - field[...]
 
         partial[...] = partial[...] - scales[0:STORED, 0:1] * dot(assemble[...], coefs)
@@ -683,8 +702,8 @@
                 pltpu.VMEM((ROWS, STORED), BF16),
                 pltpu.VMEM((STORED, 2 * ROWS), BF16),
                 pltpu.VMEM((STORED, 2 * HALO), BF16),
-                pltpu.VMEM((TIME_STEPS, HALO, 1, COLS), F32),
-                pltpu.VMEM((TIME_STEPS, HALO, 1, COLS), F32),
+                pltpu.VMEM((TIME_STEPS, MESSAGE_ROWS, 128), F32),
+                pltpu.VMEM((TIME_STEPS, MESSAGE_ROWS, 128), F32),
                 pltpu.SemaphoreType.DMA((len(operands),)),
                 pltpu.SemaphoreType.DMA((TIME_STEPS, 8)),
                 pltpu.SemaphoreType.DMA((TIME_STEPS, 8)),

time: 32.1 us -> 32.1 us (level)
  no operation moved by 1% of the time
where the time goes in v1:
time: 32.1 us; the launch traced here: 31.9 us
  Pallas kernels  31.1 us (97%)
  local copies, waits for them, and re-layouts  0.8 us (2%)
    pallas_call x1, Pallas kernels, local(): pl.pallas_call(functools.partial(kernel, rows_total), out_shape=jax.Shape...  31.1 us
    unnamed x1, local copies, waits for them, and re-layouts  0.8 us

profile of v1, /device:TPU:48, one launch (start us, length us, event | category | flops | bytes accessed | tf_op | source)
XLA Modules:
  0.0 31.9 jit_solution(6082334698337442927)
XLA Ops:
  0.0 31.1 %shard_map.100 = f32[169,768]{1,0:T(8,128)S(1)} custom-call(f32[169,768]{1,0:T(8,128)} %refs_0_.1, s32[1,169]{1,0:T(1,128)} %refs_1_.1, bf16[752,256]{1,0:T(8,128)(2,1)} %constant.8.clone.refs_2_, s32[1,9]{1,0:T(1,128)} %refs_3_.1, bf16[2048,256]{1,0:T(8,128)(2,1)} %constant.9.clone.refs_4_, bf16[9,25,768]{2,1,0:T(8,128)(2,1)} %refs_5_.1, ...), custom_call_target="tpu_custom_call" | custom-call | tf_op jit(solution)/shard_map/pallas_call | solution.py:685
  31.1 0.8 %copy.12 = f32[169,768]{1,0:T(8,128)} copy(f32[169,768]{1,0:T(8,128)S(1)} %shard_map.100) | data formatting | bytes 1038336

commit v2 on v1

--- a/solution.py
+++ b/solution.py
@@ -30,12 +30,12 @@
 
 MESSAGE_ROWS = 384
 ROUTES = (
+    (0, 1, 240, 160, 80),
+    (0, -1, 160, 240, 80),
     (1, 1, 344, 320, 8),
     (-1, 1, 336, 328, 8),
     (1, -1, 328, 336, 8),
     (-1, -1, 320, 344, 8),
-    (0, 1, 240, 160, 80),
-    (0, -1, 160, 240, 80),
     (1, 0, 80, 0, 80),
     (-1, 0, 0, 80, 80),
 )
@@ -606,18 +606,30 @@
         value = coefficients([rim_tiles(forces, c, picks) for c in range(6)], forward)
         value = jnp.where(natural < limit_col[0:EDGE_ROWS], value, 0.0)
         edges = dot(table(6), jnp.concatenate(split(value), axis=0))
-        for c in range(6):
-            values = edges[:, 128 * c : 128 * c + 128]
-            for e in range(4):
-                send[step, pl.ds(80 * e + c, SIDE, stride=6), :] = values[16 * e : 16 * e + SIDE]
-            send[step, pl.ds(320 + c, 4, stride=8), :] = values[64:68]
+        sending = exchange(step)
+
+        def pack(slots):
+            for c in range(6):
+                values = edges[:, 128 * c : 128 * c + 128]
+                for e in slots:
+                    send[step, pl.ds(80 * e + c, SIDE, stride=6), :] = values[16 * e : 16 * e + SIDE]
+
+        def start(routes):
+            for copy, goes, _ in routes:
+                pl.when(goes)(copy.start)
+
+        pack((3, 2))
 
         @pl.when(step == 0)
         def _():
             pl.semaphore_wait(barrier, expected)
 
-        for copy, goes, _ in exchange(step):
-            pl.when(goes)(copy.start)
+        start(sending[0:2])
+        for c in range(6):
+            send[step, pl.ds(320 + c, 4, stride=8), :] = edges[64:68, 128 * c : 128 * c + 128]
+        start(sending[2:6])
+        pack((1, 0))
+        start(sending[6:8])
 
         high, low = split(slabs_of(samples, MAIN, 32))
         slopes = dot(table(4), jnp.concatenate([high, high, low], axis=0))

time: 32.1 us -> 31.9 us (level)
  Pallas kernels: 31.1 us -> 30.7 us
    pallas_call x1, Pallas kernels: 31.1 us -> 30.7 us  [local(): pl.pallas_call(functools.partial(kernel, rows_total), out_shape=jax.Shape...]
where the time goes in v2:
time: 31.9 us; the launch traced here: 31.5 us
  Pallas kernels  30.7 us (96%)
  local copies, waits for them, and re-layouts  0.8 us (3%)
    pallas_call x1, Pallas kernels, local(): pl.pallas_call(functools.partial(kernel, rows_total), out_shape=jax.Shape...  30.7 us
    unnamed x1, local copies, waits for them, and re-layouts  0.8 us

profile of v2, /device:TPU:48, one launch (start us, length us, event | category | flops | bytes accessed | tf_op | source)
XLA Modules:
  0.0 31.5 jit_solution(2225172588086204473)
XLA Ops:
  0.0 30.7 %shard_map.100 = f32[169,768]{1,0:T(8,128)S(1)} custom-call(f32[169,768]{1,0:T(8,128)} %refs_0_.1, s32[1,169]{1,0:T(1,128)} %refs_1_.1, bf16[752,256]{1,0:T(8,128)(2,1)} %constant.8.clone.refs_2_, s32[1,9]{1,0:T(1,128)} %refs_3_.1, bf16[2048,256]{1,0:T(8,128)(2,1)} %constant.9.clone.refs_4_, bf16[9,25,768]{2,1,0:T(8,128)(2,1)} %refs_5_.1, ...), custom_call_target="tpu_custom_call" | custom-call | tf_op jit(solution)/shard_map/pallas_call | solution.py:697
  30.7 0.8 %copy.12 = f32[169,768]{1,0:T(8,128)} copy(f32[169,768]{1,0:T(8,128)S(1)} %shard_map.100) | data formatting | bytes 1038336

commit v3 on v2

--- a/solution.py
+++ b/solution.py
@@ -30,12 +30,12 @@
 
 MESSAGE_ROWS = 384
 ROUTES = (
-    (0, 1, 240, 160, 80),
-    (0, -1, 160, 240, 80),
     (1, 1, 344, 320, 8),
     (-1, 1, 336, 328, 8),
     (1, -1, 328, 336, 8),
     (-1, -1, 320, 344, 8),
+    (0, 1, 240, 160, 80),
+    (0, -1, 160, 240, 80),
     (1, 0, 80, 0, 80),
     (-1, 0, 0, 80, 80),
 )
@@ -85,8 +85,7 @@
 
 
 def stacked(table):
-    high, low = split_np(table)
-    return np.concatenate([high, high, low])
+    return np.concatenate(list(split_np(table)))
 
 
 def squared(table):
@@ -272,12 +271,10 @@
         first.append(both[:, 0:128] + both[:, 128:256])
     for parity in range(2):
         lanes = slice(256 + 256 * parity, 512 + 256 * parity)
-        others.append(
-            dot(
-                jnp.concatenate([high[:, lanes], low[:, lanes], high[:, lanes]], axis=1),
-                table[512 + 768 * parity : 1280 + 768 * parity, :],
-            )
-        )
+        at = 512 + 512 * parity
+        rows = high.shape[0]
+        through = dot(jnp.concatenate([high[:, lanes], low[:, lanes]], axis=0), table[at : at + 256, :])
+        others.append(through[:rows] + (through[rows:] + dot(high[:, lanes], table[at + 256 : at + 512, :])))
     return first, others
 
 
@@ -318,126 +315,18 @@
     return jnp.concatenate(tiles, axis=0)
 
 
-def slope_line(u):
-    odd0, odd1, twice = u[0] - u[4], u[1] - u[3], u[2] + u[2]
-    even0, even1 = u[0] + u[4] - twice, u[1] + u[3] - twice
-    plus, minus = [], []
-    for i in range(2):
-        plus.append(ODD[i][0] * odd0 + ODD[i][1] * odd1)
-        minus.append(EVEN[i][0] * even0 + EVEN[i][1] * even1)
-    middle = MIDDLE[0] * odd0 + MIDDLE[1] * odd1
-    return [plus[0] + minus[0], plus[1] + minus[1], middle, plus[1] - minus[1], plus[0] - minus[0]]
-
-
-def force_line(s):
-    odd0, odd1 = s[0] - s[4], s[1] - s[3]
-    even0, even1 = s[0] + s[4], s[1] + s[3]
-    plus, minus = [], []
-    for a in range(2):
-        plus.append(ODD_T[a][0] * odd0 + ODD_T[a][1] * odd1)
-        minus.append(EVEN_T[a][0] * even0 + EVEN_T[a][1] * even1 + EVEN_T[a][2] * s[2])
-    middle = MIDDLE_T[0] * odd0 + MIDDLE_T[1] * odd1
-    return [plus[0] + minus[0], plus[1] + minus[1], middle, plus[1] - minus[1], plus[0] - minus[0]]
-
-
-def by_class(value, lane):
-    kind_of_lane, early = lax.rem(lane // 2, 3), lax.rem(lane, 4) < 2
-    slabs = [value[:, 128 * v : 128 * v + 128] for v in range(6)]
-    blocks = {}
-    for kind in range(3):
-        first, second = [
-            jnp.where(
-                kind_of_lane == 0,
-                slabs[kind + 3 * h],
-                jnp.where(kind_of_lane == 1, slabs[(kind - 1) % 3 + 3 * h], slabs[(kind - 2) % 3 + 3 * h]),
-            )
-            for h in range(2)
-        ]
-        blocks[0, kind] = jnp.where(early, first, pltpu.roll(second, 2, 1))
-        blocks[1, kind] = jnp.where(early, pltpu.roll(first, 126, 1), second)
-    return jnp.concatenate([blocks[block] for block in BLOCKS], axis=1)
-
-
-def by_column(value, lane):
-    kind_of_lane, early = lax.rem(lane // 2, 3), lax.rem(lane, 4) < 2
-    blocks = {block: value[:, 128 * i : 128 * i + 128] for i, block in enumerate(BLOCKS)}
-    halves = [[], []]
-    for kind in range(3):
-        even, odd = blocks[0, kind], blocks[1, kind]
-        halves[0].append(jnp.where(early, even, pltpu.roll(odd, 2, 1)))
-        halves[1].append(jnp.where(early, pltpu.roll(even, 126, 1), odd))
-    slabs = []
-    for v in range(6):
-        parts = halves[v // 3]
-        slabs.append(
-            jnp.where(
-                kind_of_lane == 0, parts[v % 3], jnp.where(kind_of_lane == 1, parts[(v + 1) % 3], parts[(v + 2) % 3])
-            )
-        )
-    return jnp.concatenate(slabs, axis=1)
-
-
-def class_sums(high, low, table):
-    first, others = [], []
-    for parity in range(2):
-        lanes = slice(128 * parity, 128 * parity + 128)
-        both = dot(
-            jnp.concatenate([high[:, lanes], low[:, lanes]], axis=1), table[256 * parity : 256 * parity + 256, :]
-        )
-        first.append(both[:, 0:128] + both[:, 128:256])
-    for parity in range(2):
-        lanes = slice(256 + 256 * parity, 512 + 256 * parity)
-        others.append(
-            dot(
-                jnp.concatenate([high[:, lanes], low[:, lanes], high[:, lanes]], axis=1),
-                table[512 + 768 * parity : 1280 + 768 * parity, :],
-            )
-        )
-    return first, others
-
-
-def sample_blocks(bases, boths):
-    parities = []
-    for base, both in zip(bases, boths):
-        real, turned = both[:, 0:128], both[:, 128:256]
-        half = base - 0.5 * real
-        parities.append((base + real, half + turned, half - turned))
-    out = [None] * 6
-    for t in range(3):
-        out[2 * t] = parities[0][t] + parities[1][t]
-        out[(2 * t + 3) % 6] = parities[0][t] - parities[1][t]
-    return out
-
-
-def force_sums(forces):
-    out0, out12 = [], []
-    for sign in (1, -1):
-        parts = []
-        for t in range(3):
-            one, other = forces[2 * t, :, :], forces[(2 * t + 3) % 6, :, :]
-            parts.append(one + other if sign > 0 else one - other)
-        pair = parts[1] + parts[2]
-        out0.append(parts[0] + pair)
-        out12.append(jnp.concatenate([parts[0] - 0.5 * pair, parts[1] - parts[2]], axis=1))
-    return jnp.concatenate(out0, axis=1), jnp.concatenate(out12, axis=1)
-
-
 def outer_forces(samples, modulus, forces):
     def one_block(c, carry):
-        u = [samples[c, 8 * p : 8 * p + 8, :] for p in range(25)]
-        total = [None] * 25
-        for b in range(5):
-            places = [5 * a + b for a in range(5)]
-            slopes = slope_line([u[p] for p in places])
-            stress = [slopes[a] * modulus[c, 8 * p : 8 * p + 8, :] for a, p in enumerate(places)]
-            for p, part in zip(places, force_line(stress)):
-                total[p] = part
-        for a in range(5):
-            places = [5 * a + b for b in range(5)]
-            slopes = slope_line([u[p] for p in places])
-            stress = [slopes[b] * modulus[c, 8 * p : 8 * p + 8, :] for b, p in enumerate(places)]
-            for p, part in zip(places, force_line(stress)):
-                forces[c, 8 * p : 8 * p + 8, :] = total[p] + part
+        def tile(ref, p):
+            return ref[c, 8 * p : 8 * p + 8, :]
+
+        for second in range(2):
+            for i in range(5):
+                places = [5 * i + j if second else 5 * j + i for j in range(5)]
+                slopes = slope_line([tile(samples, p) for p in places])
+                parts = force_line([slope * tile(modulus, p) for slope, p in zip(slopes, places)])
+                for p, part in zip(places, parts):
+                    forces[c, 8 * p : 8 * p + 8, :] = tile(forces, p) + part if second else part
         return carry
 
     lax.fori_loop(0, 6, one_block, 0)
@@ -618,16 +507,15 @@
             for copy, goes, _ in routes:
                 pl.when(goes)(copy.start)
 
+        for c in range(6):
+            send[step, pl.ds(320 + c, 4, stride=8), :] = edges[64:68, 128 * c : 128 * c + 128]
         pack((3, 2))
 
         @pl.when(step == 0)
         def _():
             pl.semaphore_wait(barrier, expected)
 
-        start(sending[0:2])
-        for c in range(6):
-            send[step, pl.ds(320 + c, 4, stride=8), :] = edges[64:68, 128 * c : 128 * c + 128]
-        start(sending[2:6])
+        start(sending[0:6])
         pack((1, 0))
         start(sending[6:8])
 

time: 31.9 us -> 32 us (level)
    pallas_call x1, Pallas kernels: 30.7 us -> 31 us  [local(): pl.pallas_call(functools.partial(kernel, rows_total), out_shape=jax.Shape...]
where the time goes in v3:
time: 32 us; the launch traced here: 31.8 us
  Pallas kernels  31 us (97%)
  local copies, waits for them, and re-layouts  0.8 us (2%)
    pallas_call x1, Pallas kernels, local(): pl.pallas_call(functools.partial(kernel, rows_total), out_shape=jax.Shape...  31 us
    unnamed x1, local copies, waits for them, and re-layouts  0.8 us

profile of v3, /device:TPU:48, one launch (start us, length us, event | category | flops | bytes accessed | tf_op | source)
XLA Modules:
  0.0 31.8 jit_solution(13877050808918978978)
XLA Ops:
  0.0 31.0 %shard_map.100 = f32[169,768]{1,0:T(8,128)S(1)} custom-call(f32[169,768]{1,0:T(8,128)} %refs_0_.1, s32[1,169]{1,0:T(1,128)} %refs_1_.1, bf16[752,256]{1,0:T(8,128)(2,1)} %constant.8.clone.refs_2_, s32[1,9]{1,0:T(1,128)} %refs_3_.1, bf16[1536,256]{1,0:T(8,128)(2,1)} %constant.9.clone.refs_4_, bf16[9,25,768]{2,1,0:T(8,128)(2,1)} %refs_5_.1, ...), custom_call_target="tpu_custom_call" | custom-call | tf_op jit(solution)/shard_map/pallas_call | solution.py:585
  31.0 0.8 %copy.12 = f32[169,768]{1,0:T(8,128)} copy(f32[169,768]{1,0:T(8,128)S(1)} %shard_map.100) | data formatting | bytes 1038336

commit v4 on v3

--- a/solution.py
+++ b/solution.py
@@ -515,7 +515,12 @@
         def _():
             pl.semaphore_wait(barrier, expected)
 
-        start(sending[0:6])
+        even = lax.rem(me, 2) == 0
+        for copy, goes, _ in sending[4:6]:
+            pl.when(goes & even)(copy.start)
+        start(sending[0:4])
+        for copy, goes, _ in sending[4:6]:
+            pl.when(goes & jnp.logical_not(even))(copy.start)
         pack((1, 0))
         start(sending[6:8])
 

time: 32 us -> 31.8 us (level)
  Pallas kernels: 31 us -> 30.6 us
    pallas_call x1, Pallas kernels: 31 us -> 30.6 us  [local(): pl.pallas_call(functools.partial(kernel, rows_total), out_shape=jax.Shape...]
where the time goes in v4:
time: 31.8 us; the launch traced here: 31.4 us
  Pallas kernels  30.6 us (96%)
  local copies, waits for them, and re-layouts  0.8 us (3%)
    pallas_call x1, Pallas kernels, local(): pl.pallas_call(functools.partial(kernel, rows_total), out_shape=jax.Shape...  30.6 us
    unnamed x1, local copies, waits for them, and re-layouts  0.8 us

profile of v4, /device:TPU:48, one launch (start us, length us, event | category | flops | bytes accessed | tf_op | source)
XLA Modules:
  0.0 31.4 jit_solution(16601455960034464843)
XLA Ops:
  0.0 30.6 %shard_map.100 = f32[169,768]{1,0:T(8,128)S(1)} custom-call(f32[169,768]{1,0:T(8,128)} %refs_0_.1, s32[1,169]{1,0:T(1,128)} %refs_1_.1, bf16[752,256]{1,0:T(8,128)(2,1)} %constant.8.clone.refs_2_, s32[1,9]{1,0:T(1,128)} %refs_3_.1, bf16[1536,256]{1,0:T(8,128)(2,1)} %constant.9.clone.refs_4_, bf16[9,25,768]{2,1,0:T(8,128)(2,1)} %refs_5_.1, ...), custom_call_target="tpu_custom_call" | custom-call | tf_op jit(solution)/shard_map/pallas_call | solution.py:590
  30.6 0.8 %copy.12 = f32[169,768]{1,0:T(8,128)} copy(f32[169,768]{1,0:T(8,128)S(1)} %shard_map.100) | data formatting | bytes 1038336

commit v5 on v4

--- a/solution.py
+++ b/solution.py
@@ -329,7 +329,7 @@
                     forces[c, 8 * p : 8 * p + 8, :] = tile(forces, p) + part if second else part
         return carry
 
-    lax.fori_loop(0, 6, one_block, 0)
+    lax.fori_loop(0, 6, one_block, 0, unroll=2)
 
 
 def padded(ref):

time: 31.8 us -> 31.7 us (level)
  no operation moved by 1% of the time
where the time goes in v5:
time: 31.7 us; the launch traced here: 31.3 us
  Pallas kernels  30.5 us (96%)
  local copies, waits for them, and re-layouts  0.8 us (3%)
    pallas_call x1, Pallas kernels, local(): pl.pallas_call(functools.partial(kernel, rows_total), out_shape=jax.Shape...  30.5 us
    unnamed x1, local copies, waits for them, and re-layouts  0.8 us

profile of v5, /device:TPU:48, one launch (start us, length us, event | category | flops | bytes accessed | tf_op | source)
XLA Modules:
  0.0 31.3 jit_solution(15890349913220292447)
XLA Ops:
  0.0 30.5 %shard_map.100 = f32[169,768]{1,0:T(8,128)S(1)} custom-call(f32[169,768]{1,0:T(8,128)} %refs_0_.1, s32[1,169]{1,0:T(1,128)} %refs_1_.1, bf16[752,256]{1,0:T(8,128)(2,1)} %constant.8.clone.refs_2_, s32[1,9]{1,0:T(1,128)} %refs_3_.1, bf16[1536,256]{1,0:T(8,128)(2,1)} %constant.9.clone.refs_4_, bf16[9,25,768]{2,1,0:T(8,128)(2,1)} %refs_5_.1, ...), custom_call_target="tpu_custom_call" | custom-call | tf_op jit(solution)/shard_map/pallas_call | solution.py:590
  30.5 0.8 %copy.12 = f32[169,768]{1,0:T(8,128)} copy(f32[169,768]{1,0:T(8,128)S(1)} %shard_map.100) | data formatting | bytes 1038336
